TPU v7x, 32 devices: a whole 2x2x4 slice. The times are simulated.
32 devices in a mesh: groups: 2 (over y), ep: 16 (over z, x, core).
Axes of the slice: x: 2, y: 2, z: 4, core: 2. Of those that a mesh axis runs over, the one named last changes fastest.
Arguments:
- new_latent: bfloat16 [16384, 576], P(('groups', 'ep')), parts along dimension 0, may hold values from -6 to 6
- latent_gain: float32 [512], replicated, may hold values from 0.1 to 1.9
- row_slot: int32 [16384], P(('groups', 'ep')), parts along dimension 0, may hold values from 0 to 131071, as said below
- old_length: int32 [64], P(('groups', 'ep')), parts along dimension 0, may hold values from 512 to 2048, as said below
- cache: bfloat16 [64, 4096, 576], P(('groups', 'ep')), parts along dimension 0, may hold values from -6 to 6
- queries: bfloat16 [64, 2, 128, 576], P(('groups', 'ep')), parts along dimension 0, may hold values from -60 to 60
- value_up: bfloat16 [128, 512, 128], P('ep'), may hold values from -0.25 to 0.25
Outputs:
- head_values: bfloat16 [64, 2, 128, 128], P('groups', None, 'ep'), parts along dimension 0
There are 2 independent parts, one for each index of `groups`. A program takes and returns all parts, laid end to end along the dimension named above; an argument that names none is the same for every part. Nothing has to cross between parts.
Inputs may be any that keep to these rules, and one draw needn't show every extreme that they name: `row_slot`: entry i is r * 4096 + p for the request r and position p that prefill row i fills. No two rows name the same slot, p is never below old_length[r], and the rows of one device name exactly 0 or 64 slots of the requests of each owner (owner = r // 2). `old_length`: some request has exactly 2048 rows.
All inputs are finite; a program needn't handle non-finite values.
Results may differ from a plain program's by a relative error of at most 0.0059.
Values may be sent and summed in bfloat16 or wider, within the bound.
A program may use at most 64 MiB of HBM per device.

v0:
```python
import jax
import jax.numpy as jnp
from jax import lax
from jax.sharding import PartitionSpec as P


def normalize(latent_rows, gains):
    widened = latent_rows.astype(jnp.float32)
    latent_width = gains.shape[0]
    latent_part = widened[:, :latent_width]
    factor = lax.rsqrt(jnp.mean(latent_part * latent_part, axis=1, keepdims=True) + 1e-06)
    return jnp.concatenate(
        [latent_part * factor * gains[None, :], widened[:, latent_width:]], axis=1
    ).astype(jnp.bfloat16)


def masked_scores(query_rows, key_rows, usable, score_scale):
    scores = (
        lax.dot_general(
            query_rows, key_rows, (((1,), (1,)), ((), ())), preferred_element_type=jnp.float32
        )
        * score_scale
    )
    return jnp.where(usable[None, :], scores, -1e30)


def local(new_latent, latent_gain, row_slot, old_length, cache, queries, value_up):
    device_count = lax.axis_size("ep")
    req_count, cache_len, row_width = cache.shape
    latent_width = latent_gain.shape[0]
    row_count = new_latent.shape[0]
    capacity = 2 * row_count // device_count
    local_slots = req_count * cache_len
    query_count = queries.shape[1]
    head_count = queries.shape[2]
    score_scale = (value_up.shape[2] + row_width - latent_width) ** (-0.5)
    renewed = normalize(new_latent, latent_gain)
    owners = row_slot // local_slots
    belongs = (owners[:, None] == jnp.arange(device_count, dtype=jnp.int32)[None, :]).astype(
        jnp.int32
    )
    earlier = jnp.cumsum(belongs, axis=0) - belongs
    order_rank = jnp.sum(earlier * belongs, axis=1)
    target = owners * capacity + order_rank
    send_rows = (
        jnp.zeros((device_count * capacity, row_width), jnp.bfloat16).at[target].set(renewed)
    )
    send_rows = send_rows.reshape(device_count, capacity, row_width)
    send_slots = (
        jnp.full((device_count * capacity,), -1, jnp.int32)
        .at[target]
        .set(row_slot - owners * local_slots)
    )
    send_slots = send_slots.reshape(device_count, capacity)
    positions = jnp.arange(cache_len, dtype=jnp.int32)
    got_rows, got_slots = (
        lax.all_to_all(send_rows, "ep", split_axis=0, concat_axis=0, tiled=True),
        lax.all_to_all(send_slots, "ep", split_axis=0, concat_axis=0, tiled=True),
    )
    got_rows = got_rows.reshape(device_count * capacity, row_width)
    got_slots = got_slots.reshape(device_count * capacity)
    outputs = []
    old_len = cache_len // 2
    for request in range(req_count):
        query_rows = queries[request].reshape(query_count * head_count, row_width)
        old_rows = cache[request, :old_len]
        early_scores = masked_scores(
            query_rows, old_rows, positions[:old_len] < old_length[request], score_scale
        )
        owned = (got_slots >= 0) & (got_slots // cache_len == request)
        late_scores = masked_scores(query_rows, got_rows, owned, score_scale)
        highest = jnp.maximum(
            jnp.max(early_scores, axis=1, keepdims=True),
            jnp.max(late_scores, axis=1, keepdims=True),
        )
        early_weights = jnp.exp(early_scores - highest)
        late_weights = jnp.exp(late_scores - highest)
        denominator = jnp.sum(early_weights, axis=1, keepdims=True) + jnp.sum(
            late_weights, axis=1, keepdims=True
        )
        blended = jnp.dot(
            early_weights.astype(jnp.bfloat16), old_rows, preferred_element_type=jnp.float32
        )
        blended = blended + jnp.dot(
            late_weights.astype(jnp.bfloat16), got_rows, preferred_element_type=jnp.float32
        )
        blended = blended[:, :latent_width] / denominator
        outputs.append(blended.astype(jnp.bfloat16).reshape(query_count, head_count, latent_width))
    latent_out = jnp.stack(outputs, axis=0)
    return jnp.einsum(
        "rqhl,hld->rqhd",
        lax.all_to_all(latent_out, "ep", split_axis=2, concat_axis=0, tiled=True),
        value_up,
        preferred_element_type=jnp.float32,
    ).astype(jnp.bfloat16)


def solution(mesh):
    in_specs = (
        P(("groups", "ep"), None),
        P(),
        P(("groups", "ep")),
        P(("groups", "ep")),
        P(("groups", "ep"), None, None),
        P(("groups", "ep"), None, None, None),
        P("ep", None, None),
    )
    out_specs = P("groups", None, "ep", None)
    return jax.shard_map(local, mesh=mesh, in_specs=in_specs, out_specs=out_specs, check_vma=False)
```

profile of v0, /device:TPU:0, one launch (start us, length us, event | category | flops | bytes accessed | tf_op | source)
XLA Modules:
  0.0 90.0 jit_solution(11307628146478123781)
XLA Ops:
  0.0 0.8 multiply_subtract_fusion
  0.8 1.2 %reduce-window.6 = s32[16,4,128]{2,0,1:T(8,128)S(1)} reduce-window(s32[16,4,128]{2,0,1:T(8,128)S(1)} %fusion.54, s32[]{:T(128)} %constant.50.clone.1), window={size=1x1x128 pad=0_0x0_0x127_0}, to_apply=%region_1.2 | reduce-window | flops 1040384 | bytes 65540 | tf_op jit(solution)/shard_map/reduce-window
  2.3 2.4 %scatter_custom_fusion = s32[1024]{0:T(1024)S(1)} fusion(s32[512]{0:T(512)S(1)} %compare_select_fusion, s32[512]{0:T(512)S(1)} %get-tuple-element.5, s32[]{:T(128)} %constant.48.clone.1), kind=kCustom, calls=%fused_computation.96 | custom fusion | bytes 4100 | tf_op jit(solution)/shard_map/scatter | solution.py:52
  4.8 0.7 all_to_all.22
  5.4 7.4 %all-to-all-start = ((s32[16,1,64]{2,1,0:T(1,128)}), s32[16,1,64]{2,1,0:T(1,128)S(1)}, u32[]{:S(2)}, u32[]{:S(2)}) async-start(s32[16,1,64]{2,1,0:T(1,128)} %all_to_all.22), calls=%async_computation | async-start | bytes 16384 | tf_op jit(solution)/shard_map/all_to_all | solution.py:58
  12.8 1.2 %fusion.19 = f32[512]{0:T(512)S(1)} fusion(bf16[512,576]{0,1:T(8,128)(2,1)} %param.7), kind=kLoop, calls=%fused_computation.30 | loop fusion | flops 785920 | bytes 526336 | tf_op jit(solution)/shard_map/reduce_sum | solution.py:11
  14.0 0.8 slice.54
  14.9 1.2 %fusion.21 = bf16[512,512]{0,1:T(8,128)(2,1)S(1)} fusion(f32[512]{0:T(512)} %param.8, f32[512]{0:T(512)S(1)} %add_rsqrt_fusion, bf16[512,576]{0,1:T(8,128)(2,1)} %param.7), kind=kLoop, calls=%fused_computation.32 | loop fusion | flops 1048576 | bytes 1052672 | tf_op jit(solution)/shard_map/convert.2
  16.4 3.6 %scatter_custom_fusion.1 = bf16[1024,576]{1,0:T(8,128)(2,1)} fusion(s32[512]{0:T(512)S(1)} %compare_select_fusion, bf16[512,576]{1,0:T(8,128)(2,1)S(1)} %copy.18, bf16[]{:T(256)} %constant.58.clone.1), kind=kCustom, calls=%fused_computation.42 | custom fusion | bytes 1179650 | tf_op jit(solution)/shard_map/scatter | solution.py:46
  20.1 6.1 %all-to-all-start.1 = ((bf16[16,64,576]{2,1,0:T(8,128)(2,1)}), bf16[16,64,576]{2,1,0:T(8,128)(2,1)S(1)}, u32[]{:S(2)}, u32[]{:S(2)}) async-start(bf16[16,64,576]{2,1,0:T(8,128)(2,1)} %bitcast.88), calls=%async_computation.1 | async-start | bytes 2621440 | tf_op jit(solution)/shard_map/all_to_all | solution.py:57
  26.9 0.7 fusion.64
  27.6 0.7 fusion.56
  28.2 0.7 fusion.55
  28.9 4.0 %fusion.67 = (f32[256]{0:T(256)S(1)}, f32[256,2048]{1,0:T(8,128)}) fusion(bf16[2,4096,576]{1,2,0:T(8,128)(2,1)} %param.11, bf16[72,8,2,128]{3,2,1,0:T(2,128)(2,1)S(1)} %bitcast.95, pred[2048]{0:T(1024)(128)(4,1)S(1)} %fusion.56), kind=kOutput, calls=%fused_computation.103 | convolution fusion | flops 605552384 | bytes 4754432 | tf_op jit(solution)/shard_map/dot_general | solution.py:19
  32.9 4.0 %fusion.65 = (f32[256]{0:T(256)S(1)}, f32[256,2048]{1,0:T(8,128)}) fusion(bf16[2,4096,576]{1,2,0:T(8,128)(2,1)} %param.11, bf16[72,8,2,128]{3,2,1,0:T(2,128)(2,1)S(1)} %bitcast.93, pred[2048]{0:T(1024)(128)(4,1)S(1)} %fusion.55), kind=kOutput, calls=%fused_computation.101 | convolution fusion | flops 605552384 | bytes 4754432 | tf_op jit(solution)/shard_map/dot_general | solution.py:19
  37.5 0.7 reduce.9
  38.3 15.4 %all-to-all-done.1 = bf16[16,64,576]{2,1,0:T(8,128)(2,1)S(1)} async-done(((bf16[16,64,576]{2,1,0:T(8,128)(2,1)}), bf16[16,64,576]{2,1,0:T(8,128)(2,1)S(1)}, u32[]{:S(2)}, u32[]{:S(2)}) %all-to-all-start.1) | async-done | bytes 1179680 | tf_op jit(solution)/shard_map/all_to_all | solution.py:57
  55.1 0.7 copy-done.2
  56.3 2.7 %fusion.5 = f32[256,576]{1,0:T(8,128)S(1)} fusion(bf16[2,4096,576]{1,2,0:T(8,128)(2,1)} %param.11, f32[256,2048]{1,0:T(8,128)S(1)} %copy-done.2, f32[256]{0:T(256)S(1)} %max.16), kind=kOutput, calls=%fused_computation.9 | convolution fusion | flops 605028352 | bytes 5047296 | tf_op jit(solution)/shard_map/dot_general | solution.py:81
  60.5 0.7 copy-done.1
  61.6 2.7 %fusion.2 = f32[256,576]{1,0:T(8,128)S(1)} fusion(bf16[2,4096,576]{1,2,0:T(8,128)(2,1)} %param.11, f32[256,2048]{1,0:T(8,128)S(1)} %copy-done.1, f32[256]{0:T(256)S(1)} %max.17), kind=kOutput, calls=%fused_computation.6 | convolution fusion | flops 605028352 | bytes 5047296 | tf_op jit(solution)/shard_map/dot_general | solution.py:81
  65.2 0.7 pad_maximum_fusion.1
  65.9 22.3 %all_to_all.32 = bf16[2,2,128,512]{3,1,0,2:T(2,128)(2,1)S(1)} all-to-all(bf16[2,2,128,512]{3,1,0,2:T(2,128)(2,1)S(1)} %pad_maximum_fusion.1), channel_id=1, replica_groups=mesh['groups'=2,'ep'=16] {'ep'}, dimensions={2} | all-to-all | bytes 1048576 | tf_op jit(solution)/shard_map/all_to_all | solution.py:92
  89.3 0.7 copy.23
  (43 shorter events, 7.6 us)
Async XLA Ops:
  0.0 88.9 %copy-start = (bf16[8,512,128]{2,1,0:T(8,128)(2,1)S(1)}, bf16[8,512,128]{2,1,0:T(8,128)(2,1)}, u32[]{:S(2)}) copy-start(bf16[8,512,128]{2,1,0:T(8,128)(2,1)} %param.13) | copy-start | bytes 3145732
  5.4 14.6 %all-to-all-start = ((s32[16,1,64]{2,1,0:T(1,128)}), s32[16,1,64]{2,1,0:T(1,128)S(1)}, u32[]{:S(2)}, u32[]{:S(2)}) async-start(s32[16,1,64]{2,1,0:T(1,128)} %all_to_all.22), calls=%async_computation | async-start | bytes 16384 | tf_op jit(solution)/shard_map/all_to_all | solution.py:58
  16.4 9.8 %copy-start.3 = (bf16[2,2,128,576]{2,3,1,0:T(8,128)(2,1)S(1)}, bf16[2,2,128,576]{2,3,1,0:T(8,128)(2,1)}, u32[]{:S(2)}) copy-start(bf16[2,2,128,576]{2,3,1,0:T(8,128)(2,1)} %param.12) | copy-start | bytes 1769476
  20.1 6.8 %copy-start.4 = (s32[2]{0:T(128)S(1)}, s32[2]{0:T(128)}, u32[]{:S(2)}) copy-start(s32[2]{0:T(128)} %param.10) | copy-start | bytes 28
  20.1 33.6 %all-to-all-start.1 = ((bf16[16,64,576]{2,1,0:T(8,128)(2,1)}), bf16[16,64,576]{2,1,0:T(8,128)(2,1)S(1)}, u32[]{:S(2)}, u32[]{:S(2)}) async-start(bf16[16,64,576]{2,1,0:T(8,128)(2,1)} %bitcast.88), calls=%async_computation.1 | async-start | bytes 2621440 | tf_op jit(solution)/shard_map/all_to_all | solution.py:57
  54.2 1.6 %copy-start.2 = (f32[256,2048]{1,0:T(8,128)S(1)}, f32[256,2048]{1,0:T(8,128)}, u32[]{:S(2)}) copy-start(f32[256,2048]{1,0:T(8,128)} %get-tuple-element.18) | copy-start | bytes 6291460
  59.6 1.6 %copy-start.1 = (f32[256,2048]{1,0:T(8,128)S(1)}, f32[256,2048]{1,0:T(8,128)}, u32[]{:S(2)}) copy-start(f32[256,2048]{1,0:T(8,128)} %get-tuple-element.14) | copy-start | bytes 6291460
where the time goes:
time: 90.6 us; the launch traced here: 90 us
  blocking collectives  22.3 us (25%)
  matrix products  16.3 us (18%)
  waiting for transfers between devices  15.4 us (17%)
  local copies, waits for them, and re-layouts  13.5 us (15%)
  starting transfers between devices  13.5 us (15%)
  other arithmetic  8.79 us (10%)
    all_to_all x1, blocking collectives, local(): lax.all_to_all(latent_out, 'ep', split_axis=2, concat_axis=0, tiled=True)  22.3 us
    all_to_all x1, waiting for transfers between devices, local(): lax.all_to_all(send_rows, 'ep', split_axis=0, concat_axis=0, tiled=True)  15.4 us
    dot_general x4, matrix products, masked_scores(): lax.dot_general(query_rows, key_rows, (((1,), (1,)), ((), ())), preferred...  9.24 us
    all_to_all x1, starting transfers between devices, local(): lax.all_to_all(send_slots, 'ep', split_axis=0, concat_axis=0, tiled=True)  7.36 us
    all_to_all x1, starting transfers between devices, local(): lax.all_to_all(send_rows, 'ep', split_axis=0, concat_axis=0, tiled=True)  6.15 us
    dot_general x2, matrix products, local(): jnp.dot(early_weights.astype(jnp.bfloat16), old_rows, preferred_element_t...  5.49 us
    scatter x1, local copies, waits for them, and re-layouts, local(): jnp.zeros((device_count * capacity, row_width), jnp.bfloat16).at[target]  3.63 us
    scatter x1, local copies, waits for them, and re-layouts, local(): send_slots = jnp.full((device_count * capacity,), -1, jnp.int32).at[targe...  2.45 us
  transfers between devices with their start and end apart: 2, of which 1 were waited for; matrix products, arithmetic and copies ran while one was open for 21% of the time, Pallas kernels for 0%

commit v1 on v0

--- a/solution.py
+++ b/solution.py
@@ -1,7 +1,297 @@
+import functools
+
 import jax
 import jax.numpy as jnp
 from jax import lax
+from jax.experimental import pallas as pl
+from jax.experimental.pallas import tpu as pltpu
 from jax.sharding import PartitionSpec as P
+
+NT = (((1,), (1,)), ((), ()))
+LANES = 128
+TILE = 16
+MASKED = -1e30
+
+
+def flip(index, bits):
+    out, place = index, 1
+    while place <= bits:
+        if bits & place:
+            out = out + place * (1 - 2 * ((index // place) % 2))
+        place *= 2
+    return out
+
+
+def kernel(
+    dims,
+    latent_ref, gain_ref, slot_ref, length_ref, cache_ref, query_ref, up_ref,
+    out_ref,
+    renewed, send_rows, got_rows, old_rows, queries, raw_queries, up, total, highest, denom,
+    latents, got_latents,
+    row_send, row_recv, lat_send, lat_recv, own_sem, load_sem,
+):
+    n, req, cache_len, width, lat, cap, heads, qrows, scale, chunk = dims
+    me = lax.axis_index("ep")
+    hpd = heads // n
+    rope = width - lat
+    old = cache_len // 2
+    rows_req = qrows * heads
+    block = qrows * hpd
+    order = sorted(range(1, n), key=lambda k: -(k // 4 * 4)) if n >= 4 else list(range(1, n))
+    order = [k for k in order if k >= n // 2] + [k for k in order if k < n // 2]
+
+    barrier = pltpu.get_barrier_semaphore()
+    for k in range(1, n):
+        pl.semaphore_signal(
+            barrier, inc=1, device_id={"ep": flip(me, k)}, device_id_type=pl.DeviceIdType.MESH
+        )
+
+    loads = [pltpu.make_async_copy(query_ref, raw_queries, load_sem.at[0])]
+    for r in range(req):
+        loads.append(
+            pltpu.make_async_copy(
+                cache_ref.at[r, pl.ds(0, old)], old_rows.at[r], load_sem.at[1 + r]
+            )
+        )
+    loads.append(pltpu.make_async_copy(up_ref, up, load_sem.at[1 + req]))
+    for load in loads:
+        load.start()
+
+    wide = latent_ref[:, :lat].astype(jnp.float32)
+    factor = lax.rsqrt(jnp.mean(wide * wide, axis=1, keepdims=True) + 1e-06)
+    renewed[:, :lat] = (wide * factor * gain_ref[...]).astype(jnp.bfloat16)
+    count = latent_ref.shape[0]
+    renewed[:, lat:] = jnp.concatenate(
+        [
+            latent_ref[:, lat:].astype(jnp.float32),
+            jnp.zeros((count, LANES - rope), jnp.float32),
+        ],
+        axis=1,
+    ).astype(jnp.bfloat16)
+
+    slots = slot_ref[...]
+    owners = lax.div(slots, jnp.int32(req * cache_len))
+    of_request = lax.div(slots - owners * (req * cache_len), jnp.int32(cache_len))
+    belongs = (lax.broadcasted_iota(jnp.int32, (n, count), 0) == owners).astype(jnp.float32)
+    before = (
+        lax.broadcasted_iota(jnp.int32, (count, count), 0)
+        < lax.broadcasted_iota(jnp.int32, (count, count), 1)
+    ).astype(jnp.float32).astype(jnp.bfloat16)
+    earlier = jnp.dot(belongs.astype(jnp.bfloat16), before, preferred_element_type=jnp.float32)
+    rank = jnp.sum(earlier * belongs, axis=0, keepdims=True)
+    target = owners * cap + rank.astype(jnp.int32)
+    flags = (
+        lax.broadcasted_iota(jnp.int32, (LANES, count), 0) - rope == of_request
+    ).astype(jnp.float32).astype(jnp.bfloat16)
+
+    group = 4
+    part = group * cap
+    lane = lax.broadcasted_iota(jnp.int32, (part, LANES), 1)
+    flagged = (lane >= rope) & (lane < rope + req)
+
+    def fill(owner_group):
+        first = owner_group * part
+        choose = (
+            lax.broadcasted_iota(jnp.int32, (part, count), 0) + first == target
+        ).astype(jnp.float32).astype(jnp.bfloat16)
+        main = jnp.dot(choose, renewed[:, :lat], preferred_element_type=jnp.float32)
+        tail = jnp.dot(choose, renewed[:, lat:], preferred_element_type=jnp.float32)
+        mine = lax.dot_general(choose, flags, NT, preferred_element_type=jnp.float32)
+        tail = jnp.where(flagged, 1.0 - mine, tail)
+        send_rows[pl.ds(owner_group * group, group), :, :lat] = (
+            main.astype(jnp.bfloat16).reshape(group, cap, lat)
+        )
+        send_rows[pl.ds(owner_group * group, group), :, lat:] = (
+            tail.astype(jnp.bfloat16).reshape(group, cap, LANES)
+        )
+
+    def row_copy(step):
+        peer = flip(me, order[step])
+        return pltpu.make_async_remote_copy(
+            src_ref=send_rows.at[peer],
+            dst_ref=got_rows.at[step],
+            send_sem=row_send.at[step],
+            recv_sem=row_recv.at[step],
+            device_id={"ep": peer},
+            device_id_type=pl.DeviceIdType.MESH,
+        )
+
+    my_group = me // group
+    seen = []
+    for k in order + [0]:
+        if k // group not in seen:
+            seen.append(k // group)
+    for index, bits in enumerate(seen):
+        fill(flip(my_group, bits))
+        if index == 0:
+            pl.semaphore_wait(barrier, n - 1)
+        for step, k in enumerate(order):
+            if k // group == bits:
+                row_copy(step).start()
+    own_rows = pltpu.make_async_copy(send_rows.at[me], got_rows.at[n - 1], own_sem.at[0])
+    own_rows.start()
+
+    loads[0].wait()
+    for r in range(req):
+        halves, tails = [], []
+        for q in range(qrows):
+            halves.append(raw_queries[r, q, :, :lat].astype(jnp.float32).reshape(n, hpd, lat))
+            tails.append(raw_queries[r, q, :, lat:].astype(jnp.float32).reshape(n, hpd, rope))
+        main = jnp.concatenate(halves, axis=1).reshape(rows_req, lat)
+        tail = jnp.concatenate(tails, axis=1).reshape(rows_req, rope)
+        extra = lax.broadcasted_iota(jnp.int32, (rows_req, LANES - rope), 1)
+        tail = jnp.concatenate([tail, jnp.where(extra == r, MASKED, 0.0)], axis=1)
+        queries[pl.ds(r * rows_req, rows_req), :lat] = main.astype(jnp.bfloat16)
+        queries[pl.ds(r * rows_req, rows_req), lat:] = tail.astype(jnp.bfloat16)
+
+    def absorb(where, scores, values, fresh):
+        top = jnp.max(scores, axis=1, keepdims=True)
+        if not fresh:
+            was = highest[where, :1]
+            top = jnp.maximum(top, was)
+            keep = jnp.exp(was - top)
+        weights = jnp.exp(scores - top)
+        mass = jnp.sum(weights, axis=1, keepdims=True)
+        blend = jnp.dot(weights.astype(jnp.bfloat16), values, preferred_element_type=jnp.float32)
+        if not fresh:
+            mass = mass + denom[where, :1] * keep
+            blend = blend + total[where, :] * keep
+        highest[where, :] = jnp.broadcast_to(top, (top.shape[0], LANES))
+        denom[where, :] = jnp.broadcast_to(mass, (top.shape[0], LANES))
+        total[where, :] = blend
+
+    for r in range(req):
+        loads[1 + r].wait()
+        where = pl.ds(r * rows_req, rows_req)
+        limit = length_ref[r]
+
+        def early(i, fresh):
+            keys = old_rows[r, pl.ds(i * chunk, chunk), :]
+            scores = scale * lax.dot_general(
+                queries[where, :width], keys, NT, preferred_element_type=jnp.float32
+            )
+            position = i * chunk + lax.broadcasted_iota(jnp.int32, (rows_req, chunk), 1)
+            scores = jnp.where(position < limit, scores, MASKED)
+            absorb(where, scores, keys[:, :lat], fresh)
+
+        early(0, True)
+
+        @pl.loop(1, old // chunk)
+        def _(i):
+            early(i, False)
+
+    own_rows.wait()
+    groups = [list(range(n - 1))[i : i + group] for i in range(0, n - 1, group)]
+    for steps in groups:
+        for step in steps:
+            row_copy(step).wait_recv()
+        first = steps[0]
+        keys = got_rows[pl.ds(first, group)].reshape(part, lat + LANES)
+        for r in range(req):
+            where = pl.ds(r * rows_req, rows_req)
+            scores = scale * lax.dot_general(
+                queries[where, :], keys, NT, preferred_element_type=jnp.float32
+            )
+            absorb(where, scores, keys[:, :lat], False)
+
+    for r in range(req):
+        where = pl.ds(r * rows_req, rows_req)
+        latents[r] = (
+            (total[where, :] / denom[where, :1]).astype(jnp.bfloat16).reshape(n, block, lat)
+        )
+
+    def latent_copy(step):
+        peer = flip(me, order[step])
+        return pltpu.make_async_remote_copy(
+            src_ref=latents.at[:, peer],
+            dst_ref=got_latents.at[step],
+            send_sem=lat_send.at[step],
+            recv_sem=lat_recv.at[step],
+            device_id={"ep": peer},
+            device_id_type=pl.DeviceIdType.MESH,
+        )
+
+    for step in range(n - 1):
+        latent_copy(step).start()
+    own_latents = pltpu.make_async_copy(latents.at[:, me], got_latents.at[n - 1], own_sem.at[1])
+    own_latents.start()
+
+    loads[1 + req].wait()
+    for step in range(n - 1):
+        row_copy(step).wait_send()
+    own_latents.wait()
+    rows = req * block
+    head_of = lax.broadcasted_iota(jnp.int32, (group * rows, out_ref.shape[1]), 0) % hpd
+    for steps in groups:
+        for step in steps:
+            latent_copy(step).wait_recv()
+        left = got_latents[pl.ds(steps[0], group)].reshape(group * rows, lat)
+        result = jnp.zeros(head_of.shape, jnp.float32)
+        for h in range(hpd):
+            value = jnp.dot(left, up[h], preferred_element_type=jnp.float32)
+            result = jnp.where(head_of == h, value, result)
+        result = result.astype(jnp.bfloat16)
+        for i in range(group):
+            step = steps[0] + i
+            source = me if step == n - 1 else flip(me, order[step])
+            out_ref[pl.ds(source * rows, rows), :] = result[i * rows : (i + 1) * rows]
+    for step in range(n - 1):
+        latent_copy(step).wait_send()
+
+
+def fused(new_latent, latent_gain, row_slot, old_length, cache, queries, value_up):
+    n = lax.axis_size("ep")
+    req, cache_len, width = cache.shape
+    lat = latent_gain.shape[0]
+    count = new_latent.shape[0]
+    cap = 2 * count // n
+    qrows, heads = queries.shape[1:3]
+    hpd, _, hd = value_up.shape
+    scale = (hd + width - lat) ** (-0.5)
+    old = cache_len // 2
+    rows_req = qrows * heads
+    block = qrows * hpd
+    dims = (n, req, cache_len, width, lat, cap, heads, qrows, scale, min(512, old))
+    bf16, f32 = jnp.bfloat16, jnp.float32
+    vmem = pl.BlockSpec(memory_space=pltpu.VMEM)
+    hbm = pl.BlockSpec(memory_space=pl.ANY)
+    smem = pl.BlockSpec(memory_space=pltpu.SMEM)
+    wide = lat + LANES
+    out = pl.pallas_call(
+        functools.partial(kernel, dims),
+        out_shape=jax.ShapeDtypeStruct((n * req * block, hd), bf16),
+        in_specs=[vmem, vmem, vmem, smem, hbm, hbm, hbm],
+        out_specs=vmem,
+        scratch_shapes=[
+            pltpu.VMEM((count, wide), bf16),
+            pltpu.VMEM((n, cap, wide), bf16),
+            pltpu.VMEM((n, cap, wide), bf16),
+            pltpu.VMEM((req, old, width), bf16),
+            pltpu.VMEM((req * rows_req, wide), bf16),
+            pltpu.VMEM(queries.shape, bf16),
+            pltpu.VMEM(value_up.shape, bf16),
+            pltpu.VMEM((req * rows_req, lat), f32),
+            pltpu.VMEM((req * rows_req, LANES), f32),
+            pltpu.VMEM((req * rows_req, LANES), f32),
+            pltpu.VMEM((req, n, block, lat), bf16),
+            pltpu.VMEM((n, req, block, lat), bf16),
+            pltpu.SemaphoreType.DMA((n,)),
+            pltpu.SemaphoreType.DMA((n,)),
+            pltpu.SemaphoreType.DMA((n,)),
+            pltpu.SemaphoreType.DMA((n,)),
+            pltpu.SemaphoreType.DMA((2,)),
+            pltpu.SemaphoreType.DMA((req + 2,)),
+        ],
+        compiler_params=pltpu.CompilerParams(
+            collective_id=0, has_side_effects=True, vmem_limit_bytes=48 * 1024 * 1024
+        ),
+        cost_estimate=pl.CostEstimate(
+            flops=2 * req * rows_req * (old + n * cap) * (width + lat),
+            bytes_accessed=2 * req * old * width,
+            transcendentals=req * rows_req * (old + n * cap),
+        ),
+    )(new_latent, latent_gain[None, :], row_slot[None, :], old_length, cache, queries, value_up)
+    return out.reshape(n * req, qrows, hpd, hd)
 
 
 def normalize(latent_rows, gains):
@@ -24,7 +314,7 @@
     return jnp.where(usable[None, :], scores, -1e30)
 
 
-def local(new_latent, latent_gain, row_slot, old_length, cache, queries, value_up):
+def collective(new_latent, latent_gain, row_slot, old_length, cache, queries, value_up):
     device_count = lax.axis_size("ep")
     req_count, cache_len, row_width = cache.shape
     latent_width = latent_gain.shape[0]
@@ -95,6 +385,23 @@
     ).astype(jnp.bfloat16)
 
 
+def local(*args):
+    new_latent, latent_gain, _, _, cache, queries, value_up = args
+    n = lax.axis_size("ep")
+    lat = latent_gain.shape[0]
+    rope = cache.shape[2] - lat
+    whole_tiles = (
+        n % 4 == 0
+        and n & (n - 1) == 0
+        and (2 * new_latent.shape[0] // n) % TILE == 0
+        and (queries.shape[1] * value_up.shape[0]) % TILE == 0
+        and value_up.shape[0] % 8 == 0
+        and lat % LANES == 0
+        and rope + cache.shape[0] <= LANES
+    )
+    return fused(*args) if whole_tiles else collective(*args)
+
+
 def solution(mesh):
     in_specs = (
         P(("groups", "ep"), None),

time: 90.6 us -> 70.6 us (0.78)
  the two profiles are of different devices: /device:TPU:0 before, /device:TPU:17 now
where the time goes in v1:
time: 70.6 us; the launch traced here: 70.1 us
  Pallas kernels  52.9 us (75%)
  local copies, waits for them, and re-layouts  17.1 us (24%)
    pallas_call x1, Pallas kernels, fused(): pl.pallas_call(functools.partial(kernel, dims), out_shape=jax.ShapeDtypeS...  52.9 us
    unnamed x12, local copies, waits for them, and re-layouts  17.1 us

profile of v1, /device:TPU:17, one launch (start us, length us, event | category | flops | bytes accessed | tf_op | source)
XLA Modules:
  0.0 70.1 jit_solution(17163484266120264135)
XLA Ops:
  0.0 1.4 %copy.8.latent_ref = bf16[512,576]{1,0:T(8,128)(2,1)S(1)} copy(bf16[512,576]{0,1:T(8,128)(2,1)} %param.7) | data formatting | bytes 1179648 | tf_op args[0]
  1.4 0.0 copy-start
  1.4 0.0 copy-start.1
  1.4 0.0 copy-start.2
  1.4 0.0 copy-start.3
  1.4 1.4 %copy.10.query_ref = bf16[2,2,128,576]{3,2,1,0:T(8,128)(2,1)S(1)} copy(bf16[2,2,128,576]{2,3,1,0:T(8,128)(2,1)} %param.12) | data formatting | bytes 1179648 | tf_op args[5]
  2.9 13.7 %copy.9.cache_ref = bf16[2,4096,576]{2,1,0:T(8,128)(2,1)} copy(bf16[2,4096,576]{1,2,0:T(8,128)(2,1)} %param.11) | data formatting | bytes 18874368 | tf_op args[4]
  16.5 0.0 copy-done
  16.5 0.0 copy-done.1
  16.5 0.0 copy-done.2
  16.5 0.0 copy-done.3
  16.5 52.9 %shard_map.73 = bf16[512,128]{1,0:T(8,128)(2,1)S(1)} custom-call(bf16[512,576]{1,0:T(8,128)(2,1)S(1)} %copy.8.latent_ref, f32[1,512]{1,0:T(1,128)S(1)} %bitcast.4, s32[1,512]{1,0:T(1,128)S(1)} %bitcast.5, s32[2]{0:T(128)S(1)} %copy-done.3, bf16[2,4096,576]{2,1,0:T(8,128)(2,1)} %copy.9.cache_ref, bf16[2,2,128,576]{3,2,1,0:T(8,128)(2,1)S(1)} %copy.10.query_ref, ...), custom_call_target="tpu_custom_call" | custom-call | flops 3422552064 | bytes 4718592 | tf_op jit(solution)/shard_map/pallas_call | solution.py:260
  69.5 0.7 copy.12
Async XLA Ops:
  1.4 15.1 %copy-start = (bf16[8,512,128]{2,1,0:T(8,128)(2,1)S(1)}, bf16[8,512,128]{2,1,0:T(8,128)(2,1)}, u32[]{:S(2)}) copy-start(bf16[8,512,128]{2,1,0:T(8,128)(2,1)} %up_ref.1) | copy-start | bytes 3145732
  1.4 15.1 %copy-start.1 = (f32[512]{0:T(512)S(1)}, f32[512]{0:T(512)}, u32[]{:S(2)}) copy-start(f32[512]{0:T(512)} %param.8) | copy-start | bytes 6148
  1.4 15.1 %copy-start.2 = (s32[512]{0:T(512)S(1)}, s32[512]{0:T(512)}, u32[]{:S(2)}) copy-start(s32[512]{0:T(512)} %param.9) | copy-start | bytes 6148
  1.4 15.1 %copy-start.3 = (s32[2]{0:T(128)S(1)}, s32[2]{0:T(128)}, u32[]{:S(2)}) copy-start(s32[2]{0:T(128)} %length_ref.1) | copy-start | bytes 28

commit v2 on v1

--- a/solution.py
+++ b/solution.py
@@ -7,6 +7,7 @@
 from jax.experimental.pallas import tpu as pltpu
 from jax.sharding import PartitionSpec as P
 
+NN = (((1,), (0,)), ((), ()))
 NT = (((1,), (1,)), ((), ()))
 LANES = 128
 TILE = 16
@@ -50,24 +51,21 @@
     for r in range(req):
         loads.append(
             pltpu.make_async_copy(
-                cache_ref.at[r, pl.ds(0, old)], old_rows.at[r], load_sem.at[1 + r]
+                cache_ref.at[r, :, pl.ds(0, old)], old_rows.at[r], load_sem.at[1 + r]
             )
         )
     loads.append(pltpu.make_async_copy(up_ref, up, load_sem.at[1 + req]))
     for load in loads:
         load.start()
 
-    wide = latent_ref[:, :lat].astype(jnp.float32)
-    factor = lax.rsqrt(jnp.mean(wide * wide, axis=1, keepdims=True) + 1e-06)
-    renewed[:, :lat] = (wide * factor * gain_ref[...]).astype(jnp.bfloat16)
-    count = latent_ref.shape[0]
-    renewed[:, lat:] = jnp.concatenate(
-        [
-            latent_ref[:, lat:].astype(jnp.float32),
-            jnp.zeros((count, LANES - rope), jnp.float32),
-        ],
-        axis=1,
-    ).astype(jnp.bfloat16)
+    count = latent_ref.shape[1]
+    wide = latent_ref[:lat, :].astype(jnp.float32)
+    factor = lax.rsqrt(jnp.mean(wide * wide, axis=0, keepdims=True) + 1e-06)
+    gains = jnp.transpose(jnp.broadcast_to(gain_ref[...], (LANES, lat)))
+    gains = jnp.concatenate([gains] * (count // LANES), axis=1)
+    renewed[:lat, :] = (wide * factor * gains).astype(jnp.bfloat16)
+    renewed[lat:width, :] = latent_ref[lat:, :]
+    renewed[width:, :] = jnp.zeros((lat + LANES - width, count), jnp.bfloat16)
 
     slots = slot_ref[...]
     owners = lax.div(slots, jnp.int32(req * cache_len))
@@ -94,8 +92,8 @@
         choose = (
             lax.broadcasted_iota(jnp.int32, (part, count), 0) + first == target
         ).astype(jnp.float32).astype(jnp.bfloat16)
-        main = jnp.dot(choose, renewed[:, :lat], preferred_element_type=jnp.float32)
-        tail = jnp.dot(choose, renewed[:, lat:], preferred_element_type=jnp.float32)
+        main = lax.dot_general(choose, renewed[:lat, :], NT, preferred_element_type=jnp.float32)
+        tail = lax.dot_general(choose, renewed[lat:, :], NT, preferred_element_type=jnp.float32)
         mine = lax.dot_general(choose, flags, NT, preferred_element_type=jnp.float32)
         tail = jnp.where(flagged, 1.0 - mine, tail)
         send_rows[pl.ds(owner_group * group, group), :, :lat] = (
@@ -135,8 +133,9 @@
     for r in range(req):
         halves, tails = [], []
         for q in range(qrows):
-            halves.append(raw_queries[r, q, :, :lat].astype(jnp.float32).reshape(n, hpd, lat))
-            tails.append(raw_queries[r, q, :, lat:].astype(jnp.float32).reshape(n, hpd, rope))
+            turned = jnp.transpose(raw_queries[r, q].astype(jnp.float32))
+            halves.append(turned[:, :lat].reshape(n, hpd, lat))
+            tails.append(turned[:, lat:].reshape(n, hpd, rope))
         main = jnp.concatenate(halves, axis=1).reshape(rows_req, lat)
         tail = jnp.concatenate(tails, axis=1).reshape(rows_req, rope)
         extra = lax.broadcasted_iota(jnp.int32, (rows_req, LANES - rope), 1)
@@ -144,7 +143,7 @@
         queries[pl.ds(r * rows_req, rows_req), :lat] = main.astype(jnp.bfloat16)
         queries[pl.ds(r * rows_req, rows_req), lat:] = tail.astype(jnp.bfloat16)
 
-    def absorb(where, scores, values, fresh):
+    def absorb(where, scores, values, form, fresh):
         top = jnp.max(scores, axis=1, keepdims=True)
         if not fresh:
             was = highest[where, :1]
@@ -152,7 +151,9 @@
             keep = jnp.exp(was - top)
         weights = jnp.exp(scores - top)
         mass = jnp.sum(weights, axis=1, keepdims=True)
-        blend = jnp.dot(weights.astype(jnp.bfloat16), values, preferred_element_type=jnp.float32)
+        blend = lax.dot_general(
+            weights.astype(jnp.bfloat16), values, form, preferred_element_type=jnp.float32
+        )
         if not fresh:
             mass = mass + denom[where, :1] * keep
             blend = blend + total[where, :] * keep
@@ -166,13 +167,13 @@
         limit = length_ref[r]
 
         def early(i, fresh):
-            keys = old_rows[r, pl.ds(i * chunk, chunk), :]
+            keys = old_rows[r, :, pl.ds(pl.multiple_of(i * chunk, chunk), chunk)]
             scores = scale * lax.dot_general(
-                queries[where, :width], keys, NT, preferred_element_type=jnp.float32
+                queries[where, :width], keys, NN, preferred_element_type=jnp.float32
             )
             position = i * chunk + lax.broadcasted_iota(jnp.int32, (rows_req, chunk), 1)
             scores = jnp.where(position < limit, scores, MASKED)
-            absorb(where, scores, keys[:, :lat], fresh)
+            absorb(where, scores, keys[:lat, :], NT, fresh)
 
         early(0, True)
 
@@ -192,7 +193,7 @@
             scores = scale * lax.dot_general(
                 queries[where, :], keys, NT, preferred_element_type=jnp.float32
             )
-            absorb(where, scores, keys[:, :lat], False)
+            absorb(where, scores, keys[:, :lat], NN, False)
 
     for r in range(req):
         where = pl.ds(r * rows_req, rows_req)
@@ -263,12 +264,12 @@
         in_specs=[vmem, vmem, vmem, smem, hbm, hbm, hbm],
         out_specs=vmem,
         scratch_shapes=[
-            pltpu.VMEM((count, wide), bf16),
+            pltpu.VMEM((wide, count), bf16),
             pltpu.VMEM((n, cap, wide), bf16),
             pltpu.VMEM((n, cap, wide), bf16),
-            pltpu.VMEM((req, old, width), bf16),
+            pltpu.VMEM((req, width, old), bf16),
             pltpu.VMEM((req * rows_req, wide), bf16),
-            pltpu.VMEM(queries.shape, bf16),
+            pltpu.VMEM((req, qrows, width, heads), bf16),
             pltpu.VMEM(value_up.shape, bf16),
             pltpu.VMEM((req * rows_req, lat), f32),
             pltpu.VMEM((req * rows_req, LANES), f32),
@@ -290,7 +291,15 @@
             bytes_accessed=2 * req * old * width,
             transcendentals=req * rows_req * (old + n * cap),
         ),
-    )(new_latent, latent_gain[None, :], row_slot[None, :], old_length, cache, queries, value_up)
+    )(
+        new_latent.T,
+        latent_gain[None, :],
+        row_slot[None, :],
+        old_length,
+        jnp.swapaxes(cache, 1, 2),
+        jnp.swapaxes(queries, 2, 3),
+        value_up,
+    )
     return out.reshape(n * req, qrows, hpd, hd)
 
 
@@ -397,6 +406,8 @@
         and (queries.shape[1] * value_up.shape[0]) % TILE == 0
         and value_up.shape[0] % 8 == 0
         and lat % LANES == 0
+        and new_latent.shape[0] % LANES == 0
+        and queries.shape[2] % LANES == 0
         and rope + cache.shape[0] <= LANES
     )
     return fused(*args) if whole_tiles else collective(*args)

time: 70.6 us -> 59.5 us (0.84)
  the two profiles are of different devices: /device:TPU:17 before, /device:TPU:21 now
where the time goes in v2:
time: 59.5 us; the launch traced here: 59.2 us
  Pallas kernels  53.1 us (89%)
  local copies, waits for them, and re-layouts  6.03 us (10%)
    pallas_call x1, Pallas kernels, fused(): pl.pallas_call(functools.partial(kernel, dims), out_shape=jax.ShapeDtypeS...  53.1 us
    unnamed x13, local copies, waits for them, and re-layouts  6.03 us

profile of v2, /device:TPU:21, one launch (start us, length us, event | category | flops | bytes accessed | tf_op | source)
XLA Modules:
  0.0 59.2 jit_solution(11183235861502019683)
XLA Ops:
  0.0 0.0 copy-start
  0.0 1.2 %copy-done = bf16[8,512,128]{2,1,0:T(8,128)(2,1)S(1)} copy-done((bf16[8,512,128]{2,1,0:T(8,128)(2,1)S(1)}, bf16[8,512,128]{2,1,0:T(8,128)(2,1)}, u32[]{:S(2)}) %copy-start) | copy-done | bytes 1048600
  1.2 0.0 copy-start.1
  1.2 1.1 %copy-done.1 = bf16[512,576]{0,1:T(8,128)(2,1)S(1)} copy-done((bf16[512,576]{0,1:T(8,128)(2,1)S(1)}, bf16[512,576]{0,1:T(8,128)(2,1)}, u32[]{:S(2)}) %copy-start.1) | copy-done | bytes 589848
  2.3 0.0 copy-start.2
  2.3 1.1 %copy-done.2 = bf16[2,2,128,576]{2,3,1,0:T(8,128)(2,1)S(1)} copy-done((bf16[2,2,128,576]{2,3,1,0:T(8,128)(2,1)S(1)}, bf16[2,2,128,576]{2,3,1,0:T(8,128)(2,1)}, u32[]{:S(2)}) %copy-start.2) | copy-done | bytes 589848
  3.4 0.0 copy-start.3
  3.4 0.7 %copy-done.3 = f32[512]{0:T(512)S(1)} copy-done((f32[512]{0:T(512)S(1)}, f32[512]{0:T(512)}, u32[]{:S(2)}) %copy-start.3) | copy-done | bytes 2072
  4.0 0.0 copy-start.4
  4.0 0.7 %copy-done.4 = s32[512]{0:T(512)S(1)} copy-done((s32[512]{0:T(512)S(1)}, s32[512]{0:T(512)}, u32[]{:S(2)}) %copy-start.4) | copy-done | bytes 2072
  4.7 0.0 copy-start.5
  4.7 0.7 %copy-done.5 = s32[2]{0:T(128)S(1)} copy-done((s32[2]{0:T(128)S(1)}, s32[2]{0:T(128)}, u32[]{:S(2)}) %copy-start.5) | copy-done | bytes 32
  5.4 53.1 %shard_map.73 = bf16[512,128]{1,0:T(8,128)(2,1)S(1)} custom-call(bf16[576,512]{1,0:T(8,128)(2,1)S(1)} %bitcast.7, f32[1,512]{1,0:T(1,128)S(1)} %bitcast.9, s32[1,512]{1,0:T(1,128)S(1)} %bitcast.10, s32[2]{0:T(128)S(1)} %copy-done.5, bf16[2,576,4096]{2,1,0:T(8,128)(2,1)} %bitcast.11, bf16[2,2,576,128]{3,2,1,0:T(8,128)(2,1)S(1)} %bitcast.8, ...), custom_call_target="tpu_custom_call" | custom-call | flops 3422552064 | bytes 4718592 | tf_op jit(solution)/shard_map/pallas_call | solution.py:261
  58.5 0.7 %copy.9 = bf16[32,2,8,128]{3,2,1,0:T(8,128)(2,1)} copy(bf16[32,2,8,128]{3,2,1,0:T(8,128)(2,1)S(1)} %bitcast.6) | data formatting | bytes 262144
Async XLA Ops:
  0.0 1.2 %copy-start = (bf16[8,512,128]{2,1,0:T(8,128)(2,1)S(1)}, bf16[8,512,128]{2,1,0:T(8,128)(2,1)}, u32[]{:S(2)}) copy-start(bf16[8,512,128]{2,1,0:T(8,128)(2,1)} %up_ref.1) | copy-start | bytes 3145732
  1.2 1.1 %copy-start.1 = (bf16[512,576]{0,1:T(8,128)(2,1)S(1)}, bf16[512,576]{0,1:T(8,128)(2,1)}, u32[]{:S(2)}) copy-start(bf16[512,576]{0,1:T(8,128)(2,1)} %param.7) | copy-start | bytes 1769476
  2.3 1.1 %copy-start.2 = (bf16[2,2,128,576]{2,3,1,0:T(8,128)(2,1)S(1)}, bf16[2,2,128,576]{2,3,1,0:T(8,128)(2,1)}, u32[]{:S(2)}) copy-start(bf16[2,2,128,576]{2,3,1,0:T(8,128)(2,1)} %param.12) | copy-start | bytes 1769476
  3.4 0.7 %copy-start.3 = (f32[512]{0:T(512)S(1)}, f32[512]{0:T(512)}, u32[]{:S(2)}) copy-start(f32[512]{0:T(512)} %param.8) | copy-start | bytes 6148
  4.0 0.7 %copy-start.4 = (s32[512]{0:T(512)S(1)}, s32[512]{0:T(512)}, u32[]{:S(2)}) copy-start(s32[512]{0:T(512)} %param.9) | copy-start | bytes 6148
  4.7 0.7 %copy-start.5 = (s32[2]{0:T(128)S(1)}, s32[2]{0:T(128)}, u32[]{:S(2)}) copy-start(s32[2]{0:T(128)} %length_ref.1) | copy-start | bytes 28

commit v3 on v2

--- a/solution.py
+++ b/solution.py
@@ -25,11 +25,12 @@
 
 def kernel(
     dims,
-    latent_ref, gain_ref, slot_ref, length_ref, cache_ref, query_ref, up_ref,
+    latent_hbm, gain_hbm, slot_hbm, length_hbm, cache_ref, query_ref, up_ref,
     out_ref,
+    latent_ref, gain_ref, slot_ref, length_ref,
     renewed, send_rows, got_rows, old_rows, queries, raw_queries, up, total, highest, denom,
     latents, got_latents,
-    row_send, row_recv, lat_send, lat_recv, own_sem, load_sem,
+    row_send, row_recv, lat_send, lat_recv, own_sem, load_sem, small_sem,
 ):
     n, req, cache_len, width, lat, cap, heads, qrows, scale, chunk = dims
     me = lax.axis_index("ep")
@@ -38,8 +39,8 @@
     old = cache_len // 2
     rows_req = qrows * heads
     block = qrows * hpd
-    order = sorted(range(1, n), key=lambda k: -(k // 4 * 4)) if n >= 4 else list(range(1, n))
-    order = [k for k in order if k >= n // 2] + [k for k in order if k < n // 2]
+    group = 4
+    turns = list(range(n // group // 2, n // group)) + list(range(n // group // 2))[::-1]
 
     barrier = pltpu.get_barrier_semaphore()
     for k in range(1, n):
@@ -47,6 +48,19 @@
             barrier, inc=1, device_id={"ep": flip(me, k)}, device_id_type=pl.DeviceIdType.MESH
         )
 
+    smalls = [
+        pltpu.make_async_copy(source, target, small_sem.at[i])
+        for i, (source, target) in enumerate(
+            [
+                (latent_hbm, latent_ref),
+                (slot_hbm, slot_ref),
+                (gain_hbm, gain_ref),
+                (length_hbm, length_ref),
+            ]
+        )
+    ]
+    for load in smalls:
+        load.start()
     loads = [pltpu.make_async_copy(query_ref, raw_queries, load_sem.at[0])]
     for r in range(req):
         loads.append(
@@ -58,6 +72,8 @@
     for load in loads:
         load.start()
 
+    for load in smalls:
+        load.wait()
     count = latent_ref.shape[1]
     wide = latent_ref[:lat, :].astype(jnp.float32)
     factor = lax.rsqrt(jnp.mean(wide * wide, axis=0, keepdims=True) + 1e-06)
@@ -82,7 +98,6 @@
         lax.broadcasted_iota(jnp.int32, (LANES, count), 0) - rope == of_request
     ).astype(jnp.float32).astype(jnp.bfloat16)
 
-    group = 4
     part = group * cap
     lane = lax.broadcasted_iota(jnp.int32, (part, LANES), 1)
     flagged = (lane >= rope) & (lane < rope + req)
@@ -104,7 +119,7 @@
         )
 
     def row_copy(step):
-        peer = flip(me, order[step])
+        peer = flip(me, step)
         return pltpu.make_async_remote_copy(
             src_ref=send_rows.at[peer],
             dst_ref=got_rows.at[step],
@@ -115,18 +130,13 @@
         )
 
     my_group = me // group
-    seen = []
-    for k in order + [0]:
-        if k // group not in seen:
-            seen.append(k // group)
-    for index, bits in enumerate(seen):
+    for index, bits in enumerate(turns):
         fill(flip(my_group, bits))
         if index == 0:
             pl.semaphore_wait(barrier, n - 1)
-        for step, k in enumerate(order):
-            if k // group == bits:
-                row_copy(step).start()
-    own_rows = pltpu.make_async_copy(send_rows.at[me], got_rows.at[n - 1], own_sem.at[0])
+        for step in range(max(bits * group, 1), (bits + 1) * group):
+            row_copy(step).start()
+    own_rows = pltpu.make_async_copy(send_rows.at[me], got_rows.at[0], own_sem.at[0])
     own_rows.start()
 
     loads[0].wait()
@@ -182,11 +192,9 @@
             early(i, False)
 
     own_rows.wait()
-    groups = [list(range(n - 1))[i : i + group] for i in range(0, n - 1, group)]
-    for steps in groups:
-        for step in steps:
+    for first in range(0, n, group):
+        for step in range(max(first, 1), first + group):
             row_copy(step).wait_recv()
-        first = steps[0]
         keys = got_rows[pl.ds(first, group)].reshape(part, lat + LANES)
         for r in range(req):
             where = pl.ds(r * rows_req, rows_req)
@@ -202,7 +210,7 @@
         )
 
     def latent_copy(step):
-        peer = flip(me, order[step])
+        peer = flip(me, step)
         return pltpu.make_async_remote_copy(
             src_ref=latents.at[:, peer],
             dst_ref=got_latents.at[step],
@@ -212,31 +220,31 @@
             device_id_type=pl.DeviceIdType.MESH,
         )
 
-    for step in range(n - 1):
-        latent_copy(step).start()
-    own_latents = pltpu.make_async_copy(latents.at[:, me], got_latents.at[n - 1], own_sem.at[1])
+    for bits in turns:
+        for step in range(max(bits * group, 1), (bits + 1) * group):
+            latent_copy(step).start()
+    own_latents = pltpu.make_async_copy(latents.at[:, me], got_latents.at[0], own_sem.at[1])
     own_latents.start()
 
     loads[1 + req].wait()
-    for step in range(n - 1):
+    for step in range(1, n):
         row_copy(step).wait_send()
     own_latents.wait()
     rows = req * block
     head_of = lax.broadcasted_iota(jnp.int32, (group * rows, out_ref.shape[1]), 0) % hpd
-    for steps in groups:
-        for step in steps:
+    for first in range(0, n, group):
+        for step in range(max(first, 1), first + group):
             latent_copy(step).wait_recv()
-        left = got_latents[pl.ds(steps[0], group)].reshape(group * rows, lat)
+        left = got_latents[pl.ds(first, group)].reshape(group * rows, lat)
         result = jnp.zeros(head_of.shape, jnp.float32)
         for h in range(hpd):
             value = jnp.dot(left, up[h], preferred_element_type=jnp.float32)
             result = jnp.where(head_of == h, value, result)
         result = result.astype(jnp.bfloat16)
         for i in range(group):
-            step = steps[0] + i
-            source = me if step == n - 1 else flip(me, order[step])
+            source = flip(me, first + i)
             out_ref[pl.ds(source * rows, rows), :] = result[i * rows : (i + 1) * rows]
-    for step in range(n - 1):
+    for step in range(1, n):
         latent_copy(step).wait_send()
 
 
@@ -256,14 +264,17 @@
     bf16, f32 = jnp.bfloat16, jnp.float32
     vmem = pl.BlockSpec(memory_space=pltpu.VMEM)
     hbm = pl.BlockSpec(memory_space=pl.ANY)
-    smem = pl.BlockSpec(memory_space=pltpu.SMEM)
     wide = lat + LANES
     out = pl.pallas_call(
         functools.partial(kernel, dims),
         out_shape=jax.ShapeDtypeStruct((n * req * block, hd), bf16),
-        in_specs=[vmem, vmem, vmem, smem, hbm, hbm, hbm],
+        in_specs=[hbm] * 7,
         out_specs=vmem,
         scratch_shapes=[
+            pltpu.VMEM((width, count), bf16),
+            pltpu.VMEM((1, lat), f32),
+            pltpu.VMEM((1, count), jnp.int32),
+            pltpu.SMEM((req,), jnp.int32),
             pltpu.VMEM((wide, count), bf16),
             pltpu.VMEM((n, cap, wide), bf16),
             pltpu.VMEM((n, cap, wide), bf16),
@@ -282,9 +293,10 @@
             pltpu.SemaphoreType.DMA((n,)),
             pltpu.SemaphoreType.DMA((2,)),
             pltpu.SemaphoreType.DMA((req + 2,)),
+            pltpu.SemaphoreType.DMA((4,)),
         ],
         compiler_params=pltpu.CompilerParams(
-            collective_id=0, has_side_effects=True, vmem_limit_bytes=48 * 1024 * 1024
+            collective_id=0, has_side_effects=True, vmem_limit_bytes=63 * 1024 * 1024
         ),
         cost_estimate=pl.CostEstimate(
             flops=2 * req * rows_req * (old + n * cap) * (width + lat),

time: 59.5 us -> 55.1 us (0.926)
  the two profiles are of different devices: /device:TPU:21 before, /device:TPU:0 now
where the time goes in v3:
time: 55.1 us; the launch traced here: 55 us
  Pallas kernels  53.4 us (97%)
  local copies, waits for them, and re-layouts  1.57 us (3%)
    pallas_call x1, Pallas kernels, fused(): pl.pallas_call(functools.partial(kernel, dims), out_shape=jax.ShapeDtypeS...  53.4 us
    unnamed x1, local copies, waits for them, and re-layouts  1.57 us

profile of v3, /device:TPU:0, one launch (start us, length us, event | category | flops | bytes accessed | tf_op | source)
XLA Modules:
  0.0 55.0 jit_solution(18149563492805257127)
XLA Ops:
  0.0 53.4 %shard_map.73 = bf16[512,128]{1,0:T(8,128)(2,1)} custom-call(bf16[576,512]{1,0:T(8,128)(2,1)} %bitcast.8, f32[1,512]{1,0:T(1,128)} %bitcast.10, s32[1,512]{1,0:T(1,128)} %bitcast.11, s32[2]{0:T(128)} %length_hbm.1, bf16[2,576,4096]{2,1,0:T(8,128)(2,1)} %bitcast.7, bf16[2,2,576,128]{3,2,1,0:T(8,128)(2,1)} %bitcast.9, bf16[8,512,128]{2,1,0:T(8,128)(2,1)} %up_ref.1), custom_call_target="tpu_custom_call" | custom-call | flops 3422552064 | bytes 4718592 | tf_op jit(solution)/shard_map/pallas_call | solution.py:268
  53.4 1.6 %copy.9 = bf16[32,2,8,128]{3,2,1,0:T(8,128)(2,1)} copy(bf16[32,2,8,128]{3,2,1,0:T(8,128)(2,1)} %bitcast.6) | data formatting | bytes 262144

commit v4 on v3

--- a/solution.py
+++ b/solution.py
@@ -28,7 +28,7 @@
     latent_hbm, gain_hbm, slot_hbm, length_hbm, cache_ref, query_ref, up_ref,
     out_ref,
     latent_ref, gain_ref, slot_ref, length_ref,
-    renewed, send_rows, got_rows, old_rows, queries, raw_queries, up, total, highest, denom,
+    renewed, send_rows, got_rows, send_tails, got_tails, send_marks, got_marks, old_rows, queries, raw_queries, up, total, highest, denom,
     latents, got_latents,
     row_send, row_recv, lat_send, lat_recv, own_sem, load_sem, small_sem,
 ):
@@ -94,13 +94,13 @@
     earlier = jnp.dot(belongs.astype(jnp.bfloat16), before, preferred_element_type=jnp.float32)
     rank = jnp.sum(earlier * belongs, axis=0, keepdims=True)
     target = owners * cap + rank.astype(jnp.int32)
-    flags = (
-        lax.broadcasted_iota(jnp.int32, (LANES, count), 0) - rope == of_request
-    ).astype(jnp.float32).astype(jnp.bfloat16)
-
     part = group * cap
-    lane = lax.broadcasted_iota(jnp.int32, (part, LANES), 1)
-    flagged = (lane >= rope) & (lane < rope + req)
+    half = cap // 2
+    marks = jnp.broadcast_to((of_request + 1).astype(jnp.float32), (TILE, count))
+    marks = marks.astype(jnp.bfloat16)
+
+    def swap(packed):
+        return jnp.concatenate([packed[..., rope:], packed[..., :rope]], axis=-1)
 
     def fill(owner_group):
         first = owner_group * part
@@ -109,24 +109,51 @@
         ).astype(jnp.float32).astype(jnp.bfloat16)
         main = lax.dot_general(choose, renewed[:lat, :], NT, preferred_element_type=jnp.float32)
         tail = lax.dot_general(choose, renewed[lat:, :], NT, preferred_element_type=jnp.float32)
-        mine = lax.dot_general(choose, flags, NT, preferred_element_type=jnp.float32)
-        tail = jnp.where(flagged, 1.0 - mine, tail)
-        send_rows[pl.ds(owner_group * group, group), :, :lat] = (
-            main.astype(jnp.bfloat16).reshape(group, cap, lat)
-        )
-        send_rows[pl.ds(owner_group * group, group), :, lat:] = (
-            tail.astype(jnp.bfloat16).reshape(group, cap, LANES)
-        )
+        mark = lax.dot_general(marks, choose, NT, preferred_element_type=jnp.float32)
+        where = pl.ds(owner_group * group, group)
+        send_rows[where] = main.astype(jnp.bfloat16).reshape(group, cap, lat)
+        tail = tail.reshape(group, cap, LANES)
+        send_tails[where] = (tail[:, :half] + swap(tail[:, half:])).astype(jnp.bfloat16)
+        for i in range(group):
+            one = mark[:1, i * cap : (i + 1) * cap]
+            send_marks[owner_group * group + i] = jnp.concatenate([one, one], axis=1)
+
+    class Several:
+        def __init__(self, copies):
+            self.copies = copies
+
+        def start(self):
+            for copy in self.copies:
+                copy.start()
+
+        def wait(self):
+            for copy in self.copies:
+                copy.wait()
+
+        def wait_send(self):
+            for copy in self.copies:
+                copy.wait_send()
+
+        def wait_recv(self):
+            for copy in self.copies:
+                copy.wait_recv()
+
+    pairs = [(send_marks, got_marks), (send_tails, got_tails), (send_rows, got_rows)]
 
     def row_copy(step):
         peer = flip(me, step)
-        return pltpu.make_async_remote_copy(
-            src_ref=send_rows.at[peer],
-            dst_ref=got_rows.at[step],
-            send_sem=row_send.at[step],
-            recv_sem=row_recv.at[step],
-            device_id={"ep": peer},
-            device_id_type=pl.DeviceIdType.MESH,
+        return Several(
+            [
+                pltpu.make_async_remote_copy(
+                    src_ref=sent.at[peer],
+                    dst_ref=got.at[step],
+                    send_sem=row_send.at[i, step],
+                    recv_sem=row_recv.at[i, step],
+                    device_id={"ep": peer},
+                    device_id_type=pl.DeviceIdType.MESH,
+                )
+                for i, (sent, got) in enumerate(pairs)
+            ]
         )
 
     my_group = me // group
@@ -136,7 +163,12 @@
             pl.semaphore_wait(barrier, n - 1)
         for step in range(max(bits * group, 1), (bits + 1) * group):
             row_copy(step).start()
-    own_rows = pltpu.make_async_copy(send_rows.at[me], got_rows.at[0], own_sem.at[0])
+    own_rows = Several(
+        [
+            pltpu.make_async_copy(sent.at[me], got.at[0], own_sem.at[1 + i])
+            for i, (sent, got) in enumerate(pairs)
+        ]
+    )
     own_rows.start()
 
     loads[0].wait()
@@ -148,8 +180,7 @@
             tails.append(turned[:, lat:].reshape(n, hpd, rope))
         main = jnp.concatenate(halves, axis=1).reshape(rows_req, lat)
         tail = jnp.concatenate(tails, axis=1).reshape(rows_req, rope)
-        extra = lax.broadcasted_iota(jnp.int32, (rows_req, LANES - rope), 1)
-        tail = jnp.concatenate([tail, jnp.where(extra == r, MASKED, 0.0)], axis=1)
+        tail = jnp.concatenate([tail, jnp.zeros((rows_req, LANES - rope), jnp.float32)], axis=1)
         queries[pl.ds(r * rows_req, rows_req), :lat] = main.astype(jnp.bfloat16)
         queries[pl.ds(r * rows_req, rows_req), lat:] = tail.astype(jnp.bfloat16)
 
@@ -195,13 +226,25 @@
     for first in range(0, n, group):
         for step in range(max(first, 1), first + group):
             row_copy(step).wait_recv()
-        keys = got_rows[pl.ds(first, group)].reshape(part, lat + LANES)
+        packed = got_tails[pl.ds(first, group)].astype(jnp.float32)
+        tail = jnp.concatenate([packed, swap(packed)], axis=1).astype(jnp.bfloat16)
+        values = got_rows[pl.ds(first, group)].reshape(part, lat)
+        keys = jnp.concatenate([values, tail.reshape(part, LANES)], axis=1)
+        low = lax.broadcasted_iota(jnp.int32, (1, LANES), 1) < cap
+        mark = jnp.concatenate(
+            [
+                jnp.where(low, got_marks[first + i], got_marks[first + i + 1])
+                for i in range(0, group, 2)
+            ],
+            axis=1,
+        )
         for r in range(req):
             where = pl.ds(r * rows_req, rows_req)
             scores = scale * lax.dot_general(
                 queries[where, :], keys, NT, preferred_element_type=jnp.float32
             )
-            absorb(where, scores, keys[:, :lat], NN, False)
+            scores = jnp.where(mark == r + 1.0, scores, MASKED)
+            absorb(where, scores, values, NN, False)
 
     for r in range(req):
         where = pl.ds(r * rows_req, rows_req)
@@ -223,7 +266,7 @@
     for bits in turns:
         for step in range(max(bits * group, 1), (bits + 1) * group):
             latent_copy(step).start()
-    own_latents = pltpu.make_async_copy(latents.at[:, me], got_latents.at[0], own_sem.at[1])
+    own_latents = pltpu.make_async_copy(latents.at[:, me], got_latents.at[0], own_sem.at[0])
     own_latents.start()
 
     loads[1 + req].wait()
@@ -276,8 +319,12 @@
             pltpu.VMEM((1, count), jnp.int32),
             pltpu.SMEM((req,), jnp.int32),
             pltpu.VMEM((wide, count), bf16),
-            pltpu.VMEM((n, cap, wide), bf16),
-            pltpu.VMEM((n, cap, wide), bf16),
+            pltpu.VMEM((n, cap, lat), bf16),
+            pltpu.VMEM((n, cap, lat), bf16),
+            pltpu.VMEM((n, cap // 2, LANES), bf16),
+            pltpu.VMEM((n, cap // 2, LANES), bf16),
+            pltpu.VMEM((n, 1, LANES), f32),
+            pltpu.VMEM((n, 1, LANES), f32),
             pltpu.VMEM((req, width, old), bf16),
             pltpu.VMEM((req * rows_req, wide), bf16),
             pltpu.VMEM((req, qrows, width, heads), bf16),
@@ -287,11 +334,11 @@
             pltpu.VMEM((req * rows_req, LANES), f32),
             pltpu.VMEM((req, n, block, lat), bf16),
             pltpu.VMEM((n, req, block, lat), bf16),
+            pltpu.SemaphoreType.DMA((3, n)),
+            pltpu.SemaphoreType.DMA((3, n)),
             pltpu.SemaphoreType.DMA((n,)),
             pltpu.SemaphoreType.DMA((n,)),
-            pltpu.SemaphoreType.DMA((n,)),
-            pltpu.SemaphoreType.DMA((n,)),
-            pltpu.SemaphoreType.DMA((2,)),
+            pltpu.SemaphoreType.DMA((4,)),
             pltpu.SemaphoreType.DMA((req + 2,)),
             pltpu.SemaphoreType.DMA((4,)),
         ],
@@ -414,13 +461,13 @@
     whole_tiles = (
         n % 4 == 0
         and n & (n - 1) == 0
-        and (2 * new_latent.shape[0] // n) % TILE == 0
+        and 4 * new_latent.shape[0] // n == LANES
         and (queries.shape[1] * value_up.shape[0]) % TILE == 0
         and value_up.shape[0] % 8 == 0
         and lat % LANES == 0
         and new_latent.shape[0] % LANES == 0
         and queries.shape[2] % LANES == 0
-        and rope + cache.shape[0] <= LANES
+        and 2 * rope == LANES
     )
     return fused(*args) if whole_tiles else collective(*args)
 

time: 55.1 us -> 51.2 us (0.929)
  Pallas kernels: 53.4 us -> 49.5 us
    pallas_call x1, Pallas kernels: 53.4 us -> 49.5 us  [fused(): pl.pallas_call(functools.partial(kernel, dims), out_shape=jax.ShapeDtypeS...]
where the time goes in v4:
time: 51.2 us; the launch traced here: 51.1 us
  Pallas kernels  49.5 us (97%)
  local copies, waits for them, and re-layouts  1.57 us (3%)
    pallas_call x1, Pallas kernels, fused(): pl.pallas_call(functools.partial(kernel, dims), out_shape=jax.ShapeDtypeS...  49.5 us
    unnamed x1, local copies, waits for them, and re-layouts  1.57 us

profile of v4, /device:TPU:0, one launch (start us, length us, event | category | flops | bytes accessed | tf_op | source)
XLA Modules:
  0.0 51.1 jit_solution(17972314797380555119)
XLA Ops:
  0.0 49.5 %shard_map.73 = bf16[512,128]{1,0:T(8,128)(2,1)} custom-call(bf16[576,512]{1,0:T(8,128)(2,1)} %bitcast.8, f32[1,512]{1,0:T(1,128)} %bitcast.10, s32[1,512]{1,0:T(1,128)} %bitcast.11, s32[2]{0:T(128)} %length_hbm.1, bf16[2,576,4096]{2,1,0:T(8,128)(2,1)} %bitcast.7, bf16[2,2,576,128]{3,2,1,0:T(8,128)(2,1)} %bitcast.9, bf16[8,512,128]{2,1,0:T(8,128)(2,1)} %up_ref.1), custom_call_target="tpu_custom_call" | custom-call | flops 3422552064 | bytes 4718592 | tf_op jit(solution)/shard_map/pallas_call | solution.py:311
  49.5 1.6 %copy.9 = bf16[32,2,8,128]{3,2,1,0:T(8,128)(2,1)} copy(bf16[32,2,8,128]{3,2,1,0:T(8,128)(2,1)} %bitcast.6) | data formatting | bytes 262144

commit v5 on v4

--- a/solution.py
+++ b/solution.py
@@ -42,12 +42,6 @@
     group = 4
     turns = list(range(n // group // 2, n // group)) + list(range(n // group // 2))[::-1]
 
-    barrier = pltpu.get_barrier_semaphore()
-    for k in range(1, n):
-        pl.semaphore_signal(
-            barrier, inc=1, device_id={"ep": flip(me, k)}, device_id_type=pl.DeviceIdType.MESH
-        )
-
     smalls = [
         pltpu.make_async_copy(source, target, small_sem.at[i])
         for i, (source, target) in enumerate(
@@ -61,6 +55,13 @@
     ]
     for load in smalls:
         load.start()
+
+    barrier = pltpu.get_barrier_semaphore()
+    for k in range(1, n):
+        pl.semaphore_signal(
+            barrier, inc=1, device_id={"ep": flip(me, k)}, device_id_type=pl.DeviceIdType.MESH
+        )
+
     loads = [pltpu.make_async_copy(query_ref, raw_queries, load_sem.at[0])]
     for r in range(req):
         loads.append(
@@ -72,25 +73,16 @@
     for load in loads:
         load.start()
 
-    for load in smalls:
-        load.wait()
     count = latent_ref.shape[1]
-    wide = latent_ref[:lat, :].astype(jnp.float32)
-    factor = lax.rsqrt(jnp.mean(wide * wide, axis=0, keepdims=True) + 1e-06)
-    gains = jnp.transpose(jnp.broadcast_to(gain_ref[...], (LANES, lat)))
-    gains = jnp.concatenate([gains] * (count // LANES), axis=1)
-    renewed[:lat, :] = (wide * factor * gains).astype(jnp.bfloat16)
-    renewed[lat:width, :] = latent_ref[lat:, :]
-    renewed[width:, :] = jnp.zeros((lat + LANES - width, count), jnp.bfloat16)
-
+    before = (
+        lax.broadcasted_iota(jnp.int32, (count, count), 0)
+        < lax.broadcasted_iota(jnp.int32, (count, count), 1)
+    ).astype(jnp.float32).astype(jnp.bfloat16)
+    smalls[1].wait()
     slots = slot_ref[...]
     owners = lax.div(slots, jnp.int32(req * cache_len))
     of_request = lax.div(slots - owners * (req * cache_len), jnp.int32(cache_len))
     belongs = (lax.broadcasted_iota(jnp.int32, (n, count), 0) == owners).astype(jnp.float32)
-    before = (
-        lax.broadcasted_iota(jnp.int32, (count, count), 0)
-        < lax.broadcasted_iota(jnp.int32, (count, count), 1)
-    ).astype(jnp.float32).astype(jnp.bfloat16)
     earlier = jnp.dot(belongs.astype(jnp.bfloat16), before, preferred_element_type=jnp.float32)
     rank = jnp.sum(earlier * belongs, axis=0, keepdims=True)
     target = owners * cap + rank.astype(jnp.int32)
@@ -98,6 +90,16 @@
     half = cap // 2
     marks = jnp.broadcast_to((of_request + 1).astype(jnp.float32), (TILE, count))
     marks = marks.astype(jnp.bfloat16)
+
+    smalls[2].wait()
+    gains = jnp.transpose(jnp.broadcast_to(gain_ref[...], (LANES, lat)))
+    gains = jnp.concatenate([gains] * (count // LANES), axis=1)
+    smalls[0].wait()
+    wide = latent_ref[:lat, :].astype(jnp.float32)
+    factor = lax.rsqrt(jnp.mean(wide * wide, axis=0, keepdims=True) + 1e-06)
+    renewed[:lat, :] = (wide * factor * gains).astype(jnp.bfloat16)
+    renewed[lat:width, :] = latent_ref[lat:, :]
+    renewed[width:, :] = jnp.zeros((lat + LANES - width, count), jnp.bfloat16)
 
     def swap(packed):
         return jnp.concatenate([packed[..., rope:], packed[..., :rope]], axis=-1)
@@ -170,6 +172,8 @@
         ]
     )
     own_rows.start()
+
+    smalls[3].wait()
 
     loads[0].wait()
     for r in range(req):

time: 51.2 us -> 51.2 us (level)
  no operation moved by 1% of the time
where the time goes in v5:
time: 51.2 us; the launch traced here: 51.1 us
  Pallas kernels  49.5 us (97%)
  local copies, waits for them, and re-layouts  1.57 us (3%)
    pallas_call x1, Pallas kernels, fused(): pl.pallas_call(functools.partial(kernel, dims), out_shape=jax.ShapeDtypeS...  49.5 us
    unnamed x1, local copies, waits for them, and re-layouts  1.57 us

profile of v5, /device:TPU:0, one launch (start us, length us, event | category | flops | bytes accessed | tf_op | source)
XLA Modules:
  0.0 51.1 jit_solution(13109618560711827977)
XLA Ops:
  0.0 49.5 %shard_map.73 = bf16[512,128]{1,0:T(8,128)(2,1)} custom-call(bf16[576,512]{1,0:T(8,128)(2,1)} %bitcast.8, f32[1,512]{1,0:T(1,128)} %bitcast.10, s32[1,512]{1,0:T(1,128)} %bitcast.11, s32[2]{0:T(128)} %length_hbm.1, bf16[2,576,4096]{2,1,0:T(8,128)(2,1)} %bitcast.7, bf16[2,2,576,128]{3,2,1,0:T(8,128)(2,1)} %bitcast.9, bf16[8,512,128]{2,1,0:T(8,128)(2,1)} %up_ref.1), custom_call_target="tpu_custom_call" | custom-call | flops 3422552064 | bytes 4718592 | tf_op jit(solution)/shard_map/pallas_call | solution.py:315
  49.5 1.6 %copy.9 = bf16[32,2,8,128]{3,2,1,0:T(8,128)(2,1)} copy(bf16[32,2,8,128]{3,2,1,0:T(8,128)(2,1)} %bitcast.6) | data formatting | bytes 262144
